TPU v7x, 32 devices: a whole 2x2x4 slice. The times are simulated.
32 devices in a mesh: grp: 2 (over y), user: 4 (over z), tm: 4 (over x, core).
Axes of the slice: x: 2, y: 2, z: 4, core: 2. Of those that a mesh axis runs over, the one named last changes fastest.
Arguments:
- history: bfloat16 [8, 1024, 512], P(('grp', 'user'), 'tm'), parts along dimension 0, may hold values from -6 to 6
- z_weight: bfloat16 [512, 1024], replicated, may hold values from -0.25 to 0.25
- xbc_weight: bfloat16 [512, 1280], replicated, may hold values from -0.25 to 0.25
- dt_weight: bfloat16 [512, 16], replicated, may hold values from -0.125 to 0.125
- dt_bias: float32 [16], replicated, may hold values from -1 to 0.5
- a_log: float32 [16], replicated
- conv_weight: float32 [4, 1280], replicated, may hold values from -3 to 3
- conv_bias: float32 [1280], replicated, may hold values from -3 to 3
- d_skip: float32 [16], replicated, may hold values from 0.5 to 1.5
- norm_gain: float32 [1024], replicated, may hold values from 0.1 to 1.9
- out_weight: bfloat16 [1024, 512], replicated, may hold values from -0.1875 to 0.1875
- label_pos: int32 [8, 2048], P(('grp', 'user'), 'tm'), parts along dimension 0, may hold values from 0 to 1023, as said below
- label_count: int32 [8, 4], P(('grp', 'user'), 'tm'), parts along dimension 0, may hold values from 1 to 511, as said below
- label_value: int32 [8, 2048], P(('grp', 'user'), 'tm'), parts along dimension 0, may hold values 0 or 1
- item_feat: bfloat16 [8, 2048, 512], P(('grp', 'user'), 'tm'), parts along dimension 0, may hold values from -6 to 6
- first_weight: bfloat16 [1024, 1024], replicated, may hold values from -0.1875 to 0.1875
- second_weight: bfloat16 [1024], replicated, may hold values from -0.1875 to 0.1875
Outputs:
- encoded: bfloat16 [8, 1024, 512], P(('grp', 'user'), 'tm'), parts along dimension 0
- row_logit: float32 [8, 2048], P(('grp', 'user'), 'tm'), parts along dimension 0
- grad_first: float32 [2048, 1024], P('grp'), parts along dimension 0
- grad_second: float32 [2048], P('grp'), parts along dimension 0
There are 2 independent parts, one for each index of `grp`. A program takes and returns all parts, laid end to end along the dimension named above; an argument that names none is the same for every part. Nothing has to cross between parts.
Inputs may be any that keep to these rules, and one draw needn't show every extreme that they name: `label_pos`: positions in slots k * 512 to (k + 1) * 512 - 1 of a user lie in events k * 256 to (k + 1) * 256 - 1. label_count[u, k] slots are used in block k of user u's slots, and they are the block's first ones; the counts of blocks 2 * k and 2 * k + 1 of a user sum to 512.
All inputs are finite; a program needn't handle non-finite values. No bound on the sum of `label_value` on one device may be relied on, other than what follows from the above.
Results may differ from a plain program's by a relative error of at most 0.015.
Values may be sent and summed in bfloat16 or wider, within the bound.
A program may use at most 64 MiB of HBM per device.

v0:
```python
import jax
import jax.numpy as jnp
from jax import lax
from jax.sharding import PartitionSpec as P

BLOCK = 256


def passed_along(shard, axis, by):
    peers = lax.axis_size(axis)
    pairs = [(i, i + by) for i in range(peers) if 0 <= i + by < peers]
    return lax.ppermute(shard, axis, pairs)


def silu_grad(values):
    sig = jax.nn.sigmoid(values)
    return sig * (1.0 + values * (1.0 - sig))


def ranker(rank_rows, target, live_mask, first_weight, second_weight):
    pre_act = jnp.dot(rank_rows, first_weight, preferred_element_type=jnp.float32)
    hidden = jax.nn.silu(pre_act).astype(jnp.bfloat16)
    logit_vec = jnp.dot(hidden, second_weight, preferred_element_type=jnp.float32)
    dlogit = live_mask * (jax.nn.sigmoid(logit_vec) - target)
    grad_two = jnp.dot(dlogit, hidden.astype(jnp.float32), precision=lax.Precision.HIGHEST)
    grad_pre = (
        dlogit[:, None] * second_weight.astype(jnp.float32)[None, :] * silu_grad(pre_act)
    ).astype(jnp.bfloat16)
    grad_one = jnp.dot(rank_rows.T, grad_pre, preferred_element_type=jnp.float32)
    return (live_mask * logit_vec, grad_one, grad_two)


def body(
    history,
    z_weight,
    xbc_weight,
    dt_weight,
    dt_bias,
    a_log,
    conv_weight,
    conv_bias,
    d_skip,
    norm_gain,
    out_weight,
    label_pos,
    label_count,
    label_value,
    item_feat,
    first_weight,
    second_weight,
):
    user_count, length, model_width = history.shape
    inner_width = z_weight.shape[1]
    head_count = a_log.shape[0]
    head_size = inner_width // head_count
    state_dim = (xbc_weight.shape[1] - inner_width) // 2
    tap_count = conv_weight.shape[0]
    flat_rows = history.reshape(user_count * length, model_width)
    z_gate = (
        jnp.dot(flat_rows, z_weight, preferred_element_type=jnp.float32)
        .astype(jnp.bfloat16)
        .reshape(user_count, length, inner_width)
    )
    xbc_raw = (
        jnp.dot(flat_rows, xbc_weight, preferred_element_type=jnp.float32)
        .astype(jnp.bfloat16)
        .reshape(user_count, length, -1)
    )
    step_size = jax.nn.softplus(
        jnp.dot(flat_rows, dt_weight, preferred_element_type=jnp.float32) + dt_bias
    ).reshape(user_count, length, head_count)
    rim_rows = passed_along(xbc_raw[:, length - (tap_count - 1) :, :], "tm", 1)
    padded = jnp.concatenate([rim_rows, xbc_raw], axis=1)
    conv_sum = jnp.zeros(xbc_raw.shape, jnp.float32) + conv_bias
    for tap in range(tap_count):
        conv_sum = conv_sum + conv_weight[tap] * padded[:, tap : tap + length, :].astype(
            jnp.float32
        )
    xbc = jax.nn.silu(conv_sum).astype(jnp.bfloat16)
    block_count = length // BLOCK
    x_part = xbc[..., :inner_width].reshape(user_count, block_count, BLOCK, head_count, head_size)
    b_part = xbc[..., inner_width : inner_width + state_dim].reshape(
        user_count, block_count, BLOCK, state_dim
    )
    c_part = xbc[..., inner_width + state_dim :].reshape(user_count, block_count, BLOCK, state_dim)
    log_decay = (-jnp.exp(a_log) * step_size).reshape(user_count, block_count, BLOCK, head_count)
    cumulated = jnp.cumsum(log_decay, axis=2)
    step_blocks = step_size.reshape(user_count, block_count, BLOCK, head_count)
    rows_idx = lax.broadcasted_iota(jnp.int32, (BLOCK, BLOCK), 0)
    cols_idx = lax.broadcasted_iota(jnp.int32, (BLOCK, BLOCK), 1)
    causal = (cols_idx <= rows_idx)[None, None]

    def block_step(carry_state, inputs):
        x_block, b_block, c_block, cum_block, step_block = inputs
        scores = jnp.einsum("utn,usn->uts", c_block, b_block, preferred_element_type=jnp.float32)
        cum_heads = jnp.swapaxes(cum_block, 1, 2)
        gaps = cum_heads[:, :, :, None] - cum_heads[:, :, None, :]
        decays = jnp.where(causal, jnp.exp(jnp.where(causal, gaps, 0.0)), 0.0)
        weights = (decays * jnp.swapaxes(step_block, 1, 2)[:, :, None, :] * scores[:, None]).astype(
            jnp.bfloat16
        )
        within = jnp.einsum("uhts,ushp->uthp", weights, x_block, preferred_element_type=jnp.float32)
        last_cum = cum_block[:, -1, :]
        carried = (
            (jnp.exp(last_cum[:, None, :] - cum_block) * step_block)[..., None]
            * x_block.astype(jnp.float32)
        ).astype(jnp.bfloat16)
        new_state = jnp.exp(last_cum)[:, :, None, None] * carry_state + jnp.einsum(
            "ushp,usn->uhpn", carried, b_block, preferred_element_type=jnp.float32
        )
        result = within + d_skip[None, None, :, None] * x_block.astype(jnp.float32)
        return (new_state, (result, carry_state))

    zero_state = jnp.zeros((user_count, head_count, head_size, state_dim), jnp.float32)
    scan_inputs = (
        jnp.moveaxis(x_part, 1, 0),
        jnp.moveaxis(b_part, 1, 0),
        jnp.moveaxis(c_part, 1, 0),
        jnp.moveaxis(cumulated, 1, 0),
        jnp.moveaxis(step_blocks, 1, 0),
    )
    local_end, (partial_value, entering_local) = lax.scan(block_step, zero_state, scan_inputs)
    block_last = cumulated[:, :, -1, :]
    before_log = jnp.cumsum(block_last, axis=1) - block_last
    chain_gain = jnp.exp(jnp.sum(block_last, axis=1))
    incoming = jnp.zeros_like(local_end)
    for relay_step in range(lax.axis_size("tm") - 1):
        outgoing = chain_gain[:, :, None, None] * incoming + local_end
        incoming = passed_along(outgoing, "tm", 1)
    entering = (
        jnp.moveaxis(entering_local, 0, 1)
        + jnp.exp(before_log)[..., None, None] * incoming[:, None]
    )
    entering_high = entering.astype(jnp.bfloat16)
    entering_low = (entering - entering_high.astype(jnp.float32)).astype(jnp.bfloat16)
    state_read = jnp.einsum(
        "ubtn,ubhpn->ubthp", c_part, entering_high, preferred_element_type=jnp.float32
    )
    state_read = state_read + jnp.einsum(
        "ubtn,ubhpn->ubthp", c_part, entering_low, preferred_element_type=jnp.float32
    )
    across = jnp.exp(cumulated)[..., None] * state_read
    ssd_out = (jnp.moveaxis(partial_value, 0, 1) + across).reshape(user_count, length, inner_width)
    gated_out = ssd_out * jax.nn.silu(z_gate.astype(jnp.float32))
    normed = (
        gated_out
        * lax.rsqrt(jnp.mean(gated_out * gated_out, axis=-1, keepdims=True) + 1e-05)
        * norm_gain
    ).astype(jnp.bfloat16)
    encoded = (
        jnp.dot(normed.reshape(-1, inner_width), out_weight, preferred_element_type=jnp.float32)
        .astype(jnp.bfloat16)
        .reshape(user_count, length, model_width)
    )
    slot_count = label_pos.shape[1]
    tm_index = lax.axis_index("tm")
    local_pos = label_pos - tm_index * length
    enc_rows = jax.vmap(lambda table, indices: table[indices])(encoded, local_pos)
    rank_rows = jnp.concatenate([enc_rows, item_feat], axis=-1)
    slot_iota = lax.broadcasted_iota(jnp.int32, (user_count, slot_count), 1)
    live_mask = (slot_iota < label_count).astype(jnp.float32)
    target = label_value.astype(jnp.float32)
    logit_vec, grad_one, grad_two = ranker(
        rank_rows.reshape(-1, 2 * model_width),
        target.reshape(-1),
        live_mask.reshape(-1),
        first_weight,
        second_weight,
    )
    row_logit = logit_vec.reshape(user_count, slot_count)
    share_first, share_second = (
        lax.psum_scatter(
            grad_one.astype(jnp.bfloat16), "tm", scatter_dimension=0, tiled=True
        ).astype(jnp.float32),
        lax.psum_scatter(
            grad_two.astype(jnp.bfloat16), "tm", scatter_dimension=0, tiled=True
        ).astype(jnp.float32),
    )
    summed_first, summed_second = (
        lax.psum(share_first.astype(jnp.bfloat16), "user").astype(jnp.float32),
        lax.psum(share_second.astype(jnp.bfloat16), "user").astype(jnp.float32),
    )
    grad_first, grad_second = (
        lax.all_gather(summed_first.astype(jnp.bfloat16), "tm", axis=0, tiled=True).astype(
            summed_first.dtype
        ),
        lax.all_gather(summed_second.astype(jnp.bfloat16), "tm", axis=0, tiled=True).astype(
            summed_second.dtype
        ),
    )
    return (encoded, row_logit, grad_first, grad_second)


def solution(mesh):
    in_specs = (
        P(("grp", "user"), "tm", None),
        P(),
        P(),
        P(),
        P(),
        P(),
        P(),
        P(),
        P(),
        P(),
        P(),
        P(("grp", "user"), "tm"),
        P(("grp", "user"), "tm"),
        P(("grp", "user"), "tm"),
        P(("grp", "user"), "tm", None),
        P(),
        P(),
    )
    out_specs = (P(("grp", "user"), "tm", None), P(("grp", "user"), "tm"), P("grp", None), P("grp"))
    return jax.shard_map(body, mesh=mesh, in_specs=in_specs, out_specs=out_specs, check_vma=False)
```

profile of v0, /device:TPU:0, one launch (start us, length us, event | category | flops | bytes accessed | tf_op | source)
XLA Modules:
  0.0 186.5 jit_solution(1924651855535223238)
XLA Ops:
  7.3 2.0 %convolution_convert_fusion = bf16[256,1280]{1,0:T(8,128)(2,1)S(1)} fusion(bf16[512,1280]{1,0:T(8,128)(2,1)} %param.19, bf16[1,256,512]{2,1,0:T(8,128)(2,1)} %param.17), kind=kOutput, calls=%fused_computation.2 | convolution fusion | flops 335872000 | bytes 2228224 | tf_op jit(solution)/shard_map/dot_general | solution.py:65
  9.4 2.4 %collective-permute-start = (bf16[1,3,1280]{2,1,0:T(4,128)(2,1)S(1)}, bf16[1,3,1280]{2,1,0:T(4,128)(2,1)S(1)}, u32[]{:S(2)}, u32[]{:S(2)}) collective-permute-start(bf16[1,3,1280]{2,1,0:T(4,128)(2,1)S(1)} %slice.63), channel_id=1, source_target_pairs={{0,1},{1,2},{2,3},{4,5},{5,6},{6,7},{8,9},{9,10},{10,11},{12,13},{... | collective-permute-start | bytes 23048 | tf_op jit(solution)/shard_map/ppermute | solution.py:12
  14.7 2.5 %copy.42 = f32[1,256,1024]{2,1,0:T(8,128)} copy(f32[1,256,1024]{1,2,0:T(8,128)} %bitcast.132) | data formatting | bytes 2097152 | tf_op jit(solution)/shard_map/while/body/eval_jaxpr/mul | solution.py:105
  19.6 1.4 convolution_add_fusion.1
  21.9 5.3 %collective-permute-start.1 = (f32[1,16,64,128]{3,2,1,0:T(8,128)}, f32[1,16,64,128]{3,2,1,0:T(8,128)}, u32[]{:S(2)}, u32[]{:S(2)}) collective-permute-start(f32[1,16,64,128]{3,2,1,0:T(8,128)} %add_bitcast_fusion), channel_id=1, source_target_pairs={{0,1},{1,2},{2,3},{4,5},{5,6},{6,7},{8,9},{9,10},{10,11},{12,13},{... | collective-permute-start | bytes 1572872 | tf_op jit(solution)/shard_map/ppermute | solution.py:12
  28.2 2.0 %bitcast_add_fusion.2 = f32[1,16,64,128]{3,2,1,0:T(8,128)} fusion(f32[16,64,128]{2,1,0:T(8,128)S(1)} %convolution_add_fusion.1, f32[1,16,64,128]{3,2,1,0:T(8,128)} %collective-permute-done.1, f32[16]{0:T(128)S(1)} %get-tuple-element.31), kind=kLoop, calls=%fused_computation.47 | loop fusion | flops 262144 | bytes 1572928 | tf_op jit(solution)/shard_map/add | solution.py:128
  30.2 7.3 %collective-permute-start.2 = (f32[1,16,64,128]{3,2,1,0:T(8,128)}, f32[1,16,64,128]{3,2,1,0:T(8,128)}, u32[]{:S(2)}, u32[]{:S(2)}) collective-permute-start(f32[1,16,64,128]{3,2,1,0:T(8,128)} %bitcast_add_fusion.2), channel_id=1, source_target_pairs={{0,1},{1,2},{2,3},{4,5},{5,6},{6,7},{8,9},{9,10},{10,11},{12,13},{... | collective-permute-start | bytes 1572872 | tf_op jit(solution)/shard_map/ppermute | solution.py:12
  38.2 1.3 slice_convert_fusion
  39.5 2.6 %copy.41 = f32[1,256,1024]{1,2,0:T(8,128)} copy(f32[1,256,1024]{2,1,0:T(8,128)} %get-tuple-element.45) | data formatting | bytes 2097152 | tf_op jit(solution)/shard_map/while/body/eval_jaxpr/convert_element_type | solution.py:106
  42.1 2.0 %copy.37 = bf16[1,256,1024]{1,2,0:T(8,128)(2,1)} copy(bf16[1,256,1024]{2,1,0:T(8,128)(2,1)} %get-tuple-element.46) | data formatting | bytes 1048576 | tf_op jit(solution)/shard_map/slice | solution.py:81
  45.3 3.6 %collective-permute-start.3 = (f32[1,16,64,128]{3,2,1,0:T(8,128)S(1)}, f32[1,16,64,128]{3,2,1,0:T(8,128)S(1)}, u32[]{:S(2)}, u32[]{:S(2)}) collective-permute-start(f32[1,16,64,128]{3,2,1,0:T(8,128)S(1)} %bitcast_add_fusion.1), channel_id=1, source_target_pairs={{0,1},{1,2},{2,3},{4,5},{5,6},{6,7},{8,9},{9,10},{10,11},{12,13},{... | collective-permute-start | bytes 1572872 | tf_op jit(solution)/shard_map/ppermute | solution.py:12
  49.1 2.8 %fusion.11 = f32[256,16,64]{0,2,1:T(8,128)S(1)} fusion(bf16[256,16,64]{0,2,1:T(8,128)(2,1)} %bitcast.138, f32[256,256]{1,0:T(8,128)S(1)} %fusion.38, f32[16,256]{1,0:T(8,128)S(1)} %bitcast.139, f32[16,256]{1,0:T(8,128)S(1)} %bitcast.142, pred[256,256]{1,0:T(8,128)(4,1)S(1)} %iota_compare_fusion, f32[1,256,16,64]{1,3,2,0:T(8,128)} %bitcast.135, ...), kind=kOutput, calls=%fused_computation.19 | convolution fusion | flops 141033472 | bytes 2981952 | tf_op jit(solution)/shard_map/while/body/eval_jaxpr/uhts,ushp->uthp/dot_general | solution.py:102
  52.4 1.4 fusion.9
  53.8 2.5 %copy.44 = f32[256,1024]{1,0:T(8,128)} copy(f32[256,1024]{0,1:T(8,128)} %bitcast.133) | data formatting | bytes 2097152 | tf_op jit(solution)/shard_map/reshape | solution.py:143
  56.3 2.3 %multiply_reduce_fusion = (f32[256]{0:T(256)S(1)}, f32[256,1024]{1,0:T(8,128)S(1)}) fusion(f32[256,1024]{1,0:T(8,128)} %copy.44, bf16[512,1024]{1,0:T(8,128)(2,1)} %param.18, bf16[1,256,512]{2,1,0:T(8,128)(2,1)S(1)} %copy-done.4), kind=kOutput, calls=%fused_computation.38 | convolution fusion | flops 270794496 | bytes 3408896 | tf_op jit(solution)/shard_map/dot_general | solution.py:60
  59.1 5.8 %gather_fusion = bf16[512,512]{1,0:T(8,128)(2,1)} fusion(bf16[1,256,512]{2,1,0:T(8,128)(2,1)S(1)} %fusion.12, s32[512]{0:T(512)S(1)} %bitcast.129), kind=kCustom, calls=%fused_computation | custom fusion | bytes 1052672 | tf_op jit(solution)/shard_map/vmap()/gather | solution.py:158
  65.0 2.8 %multiply_convert_fusion.3 = (bf16[512,1024]{1,0:T(8,128)(2,1)S(1)}, f32[512,1024]{1,0:T(8,128)S(1)}) fusion(bf16[1024,1024]{1,0:T(8,128)(2,1)S(1)} %copy-done, bf16[1,512,512]{2,1,0:T(8,128)(2,1)} %param.31, bf16[1,512,512]{2,1,0:T(8,128)(2,1)} %bitcast.136), kind=kOutput, calls=%fused_computation.5 | convolution fusion | flops 1078460416 | bytes 6291456 | tf_op jit(solution)/shard_map/dot_general | solution.py:21
  68.8 3.0 %convolution_convert_fusion.1 = bf16[1024,1024]{1,0:T(8,128)(2,1)} fusion(f32[512,1024]{1,0:T(8,128)S(1)} %get-tuple-element.52, f32[1024]{0:T(1024)S(1)} %convert_element_type.159, f32[512]{0:T(512)S(1)} %get-tuple-element.47, bf16[1,512,512]{2,1,0:T(8,128)(2,1)S(1)} %copy-done.15, bf16[1,512,512]{2,1,0:T(8,128)(2,1)S(1)} %bitcast.137), kind=kOutput, calls=%fused_computation.13 | convolution fusion | flops 1082130432 | bytes 5249024 | tf_op jit(solution)/shard_map/dot_general | solution.py:29
  71.8 38.9 %reduce-scatter.2.cloned.1.call-done = bf16[256,1024]{1,0:T(8,128)(2,1)} async-done(((bf16[1024,1024]{1,0:T(8,128)(2,1)}), bf16[256,1024]{1,0:T(8,128)(2,1)}) %reduce-scatter.2.cloned.1.call-update) | async-done | bytes 524304 | tf_op jit(solution)/shard_map/reduce_scatter | solution.py:172
  110.9 40.7 %all-reduce.3.cloned.1.call-done = bf16[256,1024]{1,0:T(8,128)(2,1)} async-done(((bf16[256,1024]{1,0:T(8,128)(2,1)}), bf16[256,1024]{1,0:T(8,128)(2,1)}) %all-reduce.3.cloned.1.call-update) | async-done | bytes 524304 | tf_op jit(solution)/shard_map/psum | solution.py:180
  153.4 5.9 %all-reduce = bf16[1024]{0:T(1024)(128)(2,1)S(1)} all-reduce(bf16[1024]{0:T(1024)(128)(2,1)S(1)} %convert_element_type.163), channel_id=3, replica_groups=mesh['grp'=2,'user'=4,'tm'=4] {'tm'}, use_global_device_ids=true, to_apply=%region_5.6.clone | all-reduce | flops 1024 | bytes 4096
  159.3 10.5 %psum.15 = bf16[256]{0:T(256)(128)(2,1)S(1)} all-reduce(bf16[256]{0:T(256)(128)(2,1)S(1)} %dynamic-slice.4), channel_id=1, replica_groups=mesh['grp'=2,'user'=4,'tm'=4] {'user'}, use_global_device_ids=true, to_apply=%region_6.7 | all-reduce | flops 256 | bytes 1024 | tf_op jit(solution)/shard_map/psum | solution.py:181
  169.8 5.1 %all-gather = bf16[4,1,256]{2,1,0:T(2,128)(2,1)S(1)} all-gather(bf16[1,1,256]{2,1,0:T(2,128)(2,1)S(1)} %reshape.326), channel_id=1, replica_groups=mesh['grp'=2,'user'=4,'tm'=4] {'tm'}, dimensions={0}, use_global_device_ids=true | all-gather | bytes 2560 | tf_op jit(solution)/shard_map/all_gather | solution.py:187
  175.9 4.1 %convert_element_type.162 = f32[1024,1024]{1,0:T(8,128)} convert(bf16[1024,1024]{1,0:T(8,128)(2,1)} %all-gather.3.cloned.1.call-done) | non-fusion elementwise | flops 1048576 | bytes 6291456 | tf_op jit(solution)/shard_map/convert_element_type | solution.py:184
  (92 shorter events, 12.7 us)
Async XLA Ops:
  7.2 57.8 %copy-start = (bf16[1024,1024]{1,0:T(8,128)(2,1)S(1)}, bf16[1024,1024]{1,0:T(8,128)(2,1)}, u32[]{:S(2)}) copy-start(bf16[1024,1024]{1,0:T(8,128)(2,1)} %param.32) | copy-start | bytes 6291460
  7.2 4.6 %copy-start.3 = (bf16[1,256,512]{2,1,0:T(8,128)(2,1)S(1)}, bf16[1,256,512]{2,1,0:T(8,128)(2,1)}, u32[]{:S(2)}) copy-start(bf16[1,256,512]{2,1,0:T(8,128)(2,1)} %param.17) | copy-start | bytes 786436
  7.2 4.5 %copy-start.16 = (f32[16]{0:T(128)S(1)}, f32[16]{0:T(128)}, u32[]{:S(2)}) copy-start(f32[16]{0:T(128)} %param.22) | copy-start | bytes 196
  7.2 4.6 %copy-start.14 = (f32[16]{0:T(128)S(1)}, f32[16]{0:T(128)}, u32[]{:S(2)}) copy-start(f32[16]{0:T(128)} %param.21) | copy-start | bytes 196
  7.2 4.6 %copy-start.8 = (bf16[512,16]{0,1:T(8,128)(2,1)S(1)}, bf16[512,16]{0,1:T(8,128)(2,1)}, u32[]{:S(2)}) copy-start(bf16[512,16]{0,1:T(8,128)(2,1)} %param.20) | copy-start | bytes 49156
  7.2 6.3 %copy-start.7 = (f32[4,1280]{1,0:T(4,128)S(1)}, f32[4,1280]{1,0:T(4,128)}, u32[]{:S(2)}) copy-start(f32[4,1280]{1,0:T(4,128)} %param.23) | copy-start | bytes 61444
  7.2 103.6 %reduce-scatter.2.cloned.1.call-start = ((), (), s32[]{:S(2)}) async-start(), calls=%async_computation.1 | async-start | bytes 2621440 | tf_op jit(solution)/shard_map/reduce_scatter | solution.py:172
  9.3 7.9 %copy-start.9 = (f32[1280]{0:T(1024)S(1)}, f32[1280]{0:T(1024)}, u32[]{:S(2)}) copy-start(f32[1280]{0:T(1024)} %param.24) | copy-start | bytes 15364
  9.4 7.9 %collective-permute-start = (bf16[1,3,1280]{2,1,0:T(4,128)(2,1)S(1)}, bf16[1,3,1280]{2,1,0:T(4,128)(2,1)S(1)}, u32[]{:S(2)}, u32[]{:S(2)}) collective-permute-start(bf16[1,3,1280]{2,1,0:T(4,128)(2,1)S(1)} %slice.63), channel_id=1, source_target_pairs={{0,1},{1,2},{2,3},{4,5},{5,6},{6,7},{8,9},{9,10},{10,11},{12,13},{... | collective-permute-start | bytes 23048 | tf_op jit(solution)/shard_map/ppermute | solution.py:12
  18.6 8.6 %copy-start.12 = (s32[1,512]{1,0:T(1,128)S(1)}, s32[1,512]{1,0:T(1,128)}, u32[]{:S(2)}) copy-start(s32[1,512]{1,0:T(1,128)} %param.28) | copy-start | bytes 6148
  19.6 17.9 %copy-start.10 = (bf16[1024]{0:T(1024)(128)(2,1)S(1)}, bf16[1024]{0:T(1024)(128)(2,1)}, u32[]{:S(2)}) copy-start(bf16[1024]{0:T(1024)(128)(2,1)} %param.33) | copy-start | bytes 6148
  19.6 18.6 %copy-start.13 = (s32[1,512]{1,0:T(1,128)S(1)}, s32[1,512]{1,0:T(1,128)}, u32[]{:S(2)}) copy-start(s32[1,512]{1,0:T(1,128)} %param.30) | copy-start | bytes 6148
  21.9 6.4 %collective-permute-start.1 = (f32[1,16,64,128]{3,2,1,0:T(8,128)}, f32[1,16,64,128]{3,2,1,0:T(8,128)}, u32[]{:S(2)}, u32[]{:S(2)}) collective-permute-start(f32[1,16,64,128]{3,2,1,0:T(8,128)} %add_bitcast_fusion), channel_id=1, source_target_pairs={{0,1},{1,2},{2,3},{4,5},{5,6},{6,7},{8,9},{9,10},{10,11},{12,13},{... | collective-permute-start | bytes 1572872 | tf_op jit(solution)/shard_map/ppermute | solution.py:12
  30.2 13.9 %collective-permute-start.2 = (f32[1,16,64,128]{3,2,1,0:T(8,128)}, f32[1,16,64,128]{3,2,1,0:T(8,128)}, u32[]{:S(2)}, u32[]{:S(2)}) collective-permute-start(f32[1,16,64,128]{3,2,1,0:T(8,128)} %bitcast_add_fusion.2), channel_id=1, source_target_pairs={{0,1},{1,2},{2,3},{4,5},{5,6},{6,7},{8,9},{9,10},{10,11},{12,13},{... | collective-permute-start | bytes 1572872 | tf_op jit(solution)/shard_map/ppermute | solution.py:12
  39.5 9.6 %copy-start.17 = (f32[16]{0:T(128)S(1)}, f32[16]{0:T(128)}, u32[]{:S(2)}) copy-start(f32[16]{0:T(128)} %param.25) | copy-start | bytes 196
  45.3 6.7 %collective-permute-start.3 = (f32[1,16,64,128]{3,2,1,0:T(8,128)S(1)}, f32[1,16,64,128]{3,2,1,0:T(8,128)S(1)}, u32[]{:S(2)}, u32[]{:S(2)}) collective-permute-start(f32[1,16,64,128]{3,2,1,0:T(8,128)S(1)} %bitcast_add_fusion.1), channel_id=1, source_target_pairs={{0,1},{1,2},{2,3},{4,5},{5,6},{6,7},{8,9},{9,10},{10,11},{12,13},{... | collective-permute-start | bytes 1572872 | tf_op jit(solution)/shard_map/ppermute | solution.py:12
  52.3 4.0 %copy-start.4 = (bf16[1,256,512]{2,1,0:T(8,128)(2,1)S(1)}, bf16[1,256,512]{2,1,0:T(8,128)(2,1)}, u32[]{:S(2)}) copy-start(bf16[1,256,512]{2,1,0:T(8,128)(2,1)} %param.17) | copy-start | bytes 786436
  56.3 2.3 %copy-start.11 = (f32[1024]{0:T(1024)S(1)}, f32[1024]{0:T(1024)}, u32[]{:S(2)}) copy-start(f32[1024]{0:T(1024)} %param.26) | copy-start | bytes 12292
  59.1 5.8 %copy-start.1 = (bf16[1,256,512]{2,1,0:T(8,128)(2,1)}, bf16[1,256,512]{2,1,0:T(8,128)(2,1)S(1)}, u32[]{:S(2)}) copy-start(bf16[1,256,512]{2,1,0:T(8,128)(2,1)S(1)} %fusion.12) | copy-start | bytes 786436
  65.0 3.8 %copy-start.6 = (bf16[512,512]{1,0:T(8,128)(2,1)S(1)}, bf16[512,512]{1,0:T(8,128)(2,1)}, u32[]{:S(2)}) copy-start(bf16[512,512]{1,0:T(8,128)(2,1)} %gather_fusion) | copy-start | bytes 1572868
  65.0 3.8 %copy-start.15 = (bf16[1,512,512]{2,1,0:T(8,128)(2,1)S(1)}, bf16[1,512,512]{2,1,0:T(8,128)(2,1)}, u32[]{:S(2)}) copy-start(bf16[1,512,512]{2,1,0:T(8,128)(2,1)} %param.31) | copy-start | bytes 1572868
  71.8 79.8 %copy-start.18 = (u32[32]{0:T(128)S(1)}, u32[32]{0:T(128)}, u32[]{:S(2)}) copy-start(u32[32]{0:T(128)} %constant.78) | copy-start | bytes 388
  71.8 79.8 %all-reduce.3.cloned.1.call-start = ((), (), s32[]{:S(2)}) async-start(), calls=%async_computation.2 | async-start | bytes 1048576 | tf_op jit(solution)/shard_map/psum | solution.py:180
  110.8 65.0 %all-gather.3.cloned.1.call-start = ((), (), s32[]{:S(2)}) async-start(), calls=%async_computation.3 | async-start | bytes 2621440 | tf_op jit(solution)/shard_map/all_gather | solution.py:184
  (2 other events, 3.5 us)
Sparse Core Ops, SparseCore 0:
  71.9 38.8 reduce-scatter.1
  113.3 38.2 all-reduce.2
  153.2 22.5 all-gather.2
where the time goes:
time: 187 us; the launch traced here: 186 us
  waiting for transfers between devices  81.1 us (43%)
  blocking collectives  21.4 us (11%)
  local copies, waits for them, and re-layouts  19.2 us (10%)
  starting transfers between devices  18.7 us (10%)
  matrix products  17.8 us (10%)
  between operations  15.4 us (8%)
  other arithmetic  12.8 us (7%)
    psum x1, waiting for transfers between devices, body(): lax.psum(share_first.astype(jnp.bfloat16), 'user').astype(jnp.float32)  40.7 us
    reduce_scatter x1, waiting for transfers between devices, body(): lax.psum_scatter(grad_one.astype(jnp.bfloat16), 'tm', scatter_dimension=0...  38.9 us
    ppermute x4, starting transfers between devices, passed_along(): return lax.ppermute(shard, axis, pairs)  18.6 us
    psum x1, blocking collectives, body(): lax.psum(share_second.astype(jnp.bfloat16), 'user').astype(jnp.float32)  10.5 us
    unnamed x1, blocking collectives  5.85 us
    gather x2, local copies, waits for them, and re-layouts, body(): table[indices]  5.84 us
    all_gather x1, blocking collectives, body(): lax.all_gather(summed_second.astype(jnp.bfloat16), 'tm', axis=0, tiled=True)  5.06 us
    convert_element_type x1, other arithmetic, body(): lax.all_gather(summed_first.astype(jnp.bfloat16), 'tm', axis=0, tiled=True)  4.07 us
  transfers between devices with their start and end apart: 7, of which 4 were waited for; matrix products, arithmetic and copies ran while one was open for 9% of the time, Pallas kernels for 0%

commit v1 on v0

v1 whole, which is shorter than its diff:
```python
import functools

import jax
import jax.numpy as jnp
from jax import lax
from jax.experimental import pallas as pl
from jax.experimental.pallas import tpu as pltpu
from jax.sharding import PartitionSpec as P

F32, BF16 = jnp.float32, jnp.bfloat16
MESH = pl.DeviceIdType.MESH
HIGH = lax.Precision.HIGHEST
TILE = 256
RB = 16


def dot(a, b, dims=((1,), (0,)), precision=None):
    return lax.dot_general(a, b, (dims, ((), ())), preferred_element_type=F32, precision=precision)


def sigmoid(v):
    return jax.nn.sigmoid(v)


def run_all(streams):
    live = list(streams)
    while live:
        for s in list(live):
            try:
                next(s)
            except StopIteration:
                live.remove(s)


def kernel(
    nt, nu, head_count,
    hist, zw, xw, dtw, dtb, alog, cw, cb, dsk, ng, ow, pos, cnt, lab, item, fw, sw,
    enc_o, logit_o, res, g2_o,
    hv, zv, xv, ov, rr, fv, rim, rawf, xb, zb, y, ea, eb, car, sl, st_in, st_out, nb,
    pa, hb, gp, ltb, g, rc, ax_r, ax_l, az_r, az_l, bz_r, bz_l, bx_r, bx_l, s2, s2t, s2u,
    ld_sem, rim_sem, st_sem, pair_sem, rs_sem, ag_sem, s2_sem,
):
    nx = nt // 2
    tm, us = lax.axis_index("tm"), lax.axis_index("user")
    xi, core = tm // 2, tm % 2
    partner = tm + 1 - 2 * core
    rows, width = hist.shape
    inner = zw.shape[1]
    state = (xw.shape[1] - inner) // 2
    head_size = inner // head_count
    slots, hid = item.shape[0], fw.shape[1]
    tiles = inner // TILE
    htiles = hid // TILE

    loads = [
        pltpu.make_async_copy(s, d, ld_sem.at[i])
        for i, (s, d) in enumerate(
            ((hist, hv), (xw, xv), (zw, zv), (fw, fv), (item, rr.at[:, width:]), (ow, ov))
        )
    ]
    for c in loads:
        c.start()

    barrier = pltpu.get_barrier_semaphore()
    for d in range(1, nt):
        pl.semaphore_signal(barrier, inc=1, device_id={"tm": (tm + d) % nt}, device_id_type=MESH)
    for d in range(1, nu):
        pl.semaphore_signal(barrier, inc=1, device_id={"user": (us + d) % nu}, device_id_type=MESH)
    pl.semaphore_wait(barrier, nt + nu - 2)

    def remote(src, dst, ssem, rsem, dev):
        return pltpu.make_async_remote_copy(
            src_ref=src, dst_ref=dst, send_sem=ssem, recv_sem=rsem, device_id=dev, device_id_type=MESH
        )

    loads[0].wait()
    rim_copy = remote(
        hv.at[pl.ds(rows - 16, 16)], rim, rim_sem.at[0], rim_sem.at[1], {"tm": (tm + 1) % nt}
    )

    @pl.when(tm < nt - 1)
    def _():
        rim_copy.start()

    @pl.when(tm == 0)
    def _():
        rim[...] = jnp.zeros_like(rim)
        st_in[...] = jnp.zeros_like(st_in)

    v = dot(hv[...], dtw[...]) + dtb[...]
    dt = jnp.maximum(v, 0.0) + jnp.log1p(jnp.exp(-jnp.abs(v)))
    log_decay = -jnp.exp(alog[...]) * dt
    ri = lax.broadcasted_iota(jnp.int32, (rows, rows), 0)
    ci = lax.broadcasted_iota(jnp.int32, (rows, rows), 1)
    tri = jnp.where(ci <= ri, 1.0, 0.0).astype(F32)
    eye = jnp.where(ci == ri, 1.0, 0.0).astype(F32)
    cum = dot(tri, log_decay, precision=HIGH)
    cum_t = dot(log_decay, tri, ((0,), (1,)), HIGH)
    dt_t = dot(dt, eye, ((0,), (0,)), HIGH)
    eh = lax.broadcasted_iota(jnp.int32, (head_count, inner), 0) * head_size
    ec = lax.broadcasted_iota(jnp.int32, (head_count, inner), 1)
    spread = jnp.where((ec >= eh) & (ec < eh + head_size), 1.0, 0.0).astype(F32)
    last = cum[rows - 1 : rows, :]
    ea[...] = dot(jnp.exp(cum), spread, precision=HIGH)
    eb[...] = dot(jnp.exp(last - cum) * dt, spread, precision=HIGH)
    skip = dot(jnp.broadcast_to(dsk[...], (8, head_count)), spread, precision=HIGH)[0:1]

    loads[1].wait()

    @pl.loop(0, xw.shape[1] // TILE)
    def _(j):
        cols = pl.ds(pl.multiple_of(j * TILE, TILE), TILE)
        rawf[pl.ds(8, rows), cols] = dot(hv[...], xv[:, cols]).astype(BF16).astype(F32)

    @pl.when(tm > 0)
    def _():
        rim_copy.wait_recv()

    @pl.loop(0, xw.shape[1] // TILE)
    def _(j):
        cols = pl.ds(pl.multiple_of(j * TILE, TILE), TILE)
        edge = dot(rim[...], xv[:, cols]).astype(BF16).astype(F32)
        rawf[pl.ds(0, 8), cols] = edge[8:16]
        taps = cw.shape[0]
        acc = jnp.broadcast_to(cb[:, cols], (rows, TILE))
        for k in range(taps):
            acc = acc + cw[pl.ds(k, 1), cols] * rawf[pl.ds(8 - (taps - 1) + k, rows), cols]
        xb[:, cols] = (acc * sigmoid(acc)).astype(BF16)

    b_part = xb[:, inner : inner + state]
    c_part = xb[:, inner + state :]
    for j in range(tiles):
        cols = slice(j * TILE, (j + 1) * TILE)
        car[:, cols] = (eb[:, cols] * xb[:, cols].astype(F32)).astype(BF16)
        sl[j] = dot(b_part, car[:, cols], ((0,), (0,)))

    def st_copy(j):
        return remote(st_out.at[j], st_in.at[j], st_sem.at[0, j], st_sem.at[1, j], {"tm": (tm + 1) % nt})

    def relay():
        for j in range(tiles):
            @pl.when(tm > 0)
            def _():
                st_copy(j).wait_recv()

            @pl.when(tm < nt - 1)
            def _():
                gain = ea[rows - 1 : rows, j * TILE : (j + 1) * TILE]
                st_out[j] = (gain * st_in[j].astype(F32) + sl[j]).astype(BF16)
                st_copy(j).start()

    @pl.when(tm == 0)
    def _():
        relay()

    scores = jnp.where(ci <= ri, dot(c_part, b_part, ((1,), (1,))), 0.0)
    per = 128 // head_size
    lane = lax.broadcasted_iota(jnp.int32, (rows, 128), 1)
    groups = inner // 128
    for q in range(groups):
        xp = xb[:, q * 128 : (q + 1) * 128]
        out = jnp.zeros((rows, 128), F32)
        for r in range(per):
            h = q * per + r
            gap = jnp.minimum(cum[:, h : h + 1] - cum_t[h : h + 1, :], 0.0)
            w = (jnp.exp(gap) * dt_t[h : h + 1, :] * scores).astype(BF16)
            out = jnp.where(lane >= r * head_size, dot(w, xp), out)
        y[:, q * 128 : (q + 1) * 128] = out
        if q == groups // 4:
            @pl.when(tm == 1)
            def _():
                relay()

    loads[2].wait()

    @pl.loop(0, tiles)
    def _(j):
        cols = pl.ds(pl.multiple_of(j * TILE, TILE), TILE)
        zb[:, cols] = dot(hv[...], zv[:, cols]).astype(BF16)

    loads[3].wait()
    loads[4].wait()

    @pl.loop(0, htiles)
    def _(j):
        cols = pl.ds(pl.multiple_of(j * TILE, TILE), TILE)
        pa[:, cols] = dot(rr[:, width:], fv[width:, cols])

    @pl.when(tm > 1)
    def _():
        relay()

    square = jnp.zeros((rows, 1), F32)
    for j in range(tiles):
        cols = slice(j * TILE, (j + 1) * TILE)
        across = ea[:, cols] * dot(c_part, st_in[j])
        zf = zb[:, cols].astype(F32)
        gated = (y[:, cols] + across + skip[:, cols] * xb[:, cols].astype(F32)) * (zf * sigmoid(zf))
        y[:, cols] = gated
        square = square + jnp.sum(gated * gated, axis=1, keepdims=True)
    scale = lax.rsqrt(square / inner + 1e-05)
    for j in range(tiles):
        cols = slice(j * TILE, (j + 1) * TILE)
        nb[:, cols] = (y[:, cols] * scale * ng[:, cols]).astype(BF16)
    loads[5].wait()

    @pl.loop(0, width // TILE)
    def _(j):
        cols = pl.ds(pl.multiple_of(j * TILE, TILE), TILE)
        enc_o[:, cols] = dot(nb[...], ov[:, cols]).astype(BF16)

    local = pos[...] - tm * rows
    pick = lax.broadcasted_iota(jnp.int32, (rows, slots), 0) == local
    pick = jnp.where(pick, 1.0, 0.0).astype(BF16)
    rr[:, :width] = dot(pick, enc_o[...], ((0,), (0,))).astype(BF16)

    @pl.loop(0, htiles)
    def _(j):
        cols = pl.ds(pl.multiple_of(j * TILE, TILE), TILE)
        p = pa[:, cols] + dot(rr[:, :width], fv[:width, cols])
        pa[:, cols] = p
        hb[:, cols] = (p * sigmoid(p)).astype(BF16)

    logit = dot(jnp.broadcast_to(sw[...], (16, hid)), hb[...], ((1,), (1,)))[0:1]
    live = (lax.broadcasted_iota(jnp.int32, (1, slots), 1) < cnt[...]).astype(F32)
    logit_o[...] = live * logit
    dl = live * (sigmoid(logit) - lab[...].astype(F32))
    d1 = dl.astype(BF16).astype(F32)
    d2 = (dl - d1).astype(BF16).astype(F32)
    d3 = dl - d1 - d2
    ki = lax.broadcasted_iota(jnp.int32, (16, slots), 0)
    lhs = jnp.where(ki == 0, d1, jnp.where(ki == 1, d2, jnp.where(ki == 2, d3, 0.0))).astype(BF16)
    second = jnp.sum(dot(lhs, hb[...]), axis=0, keepdims=True)
    for j in range(hid // 128):
        s2[j : j + 1, :] = second[:, j * 128 : (j + 1) * 128]
    s2_copies = [
        remote(s2, s2t.at[d - 1], s2_sem.at[0, d - 1], s2_sem.at[1, d - 1], {"tm": (tm + d) % nt})
        for d in range(1, nt)
    ]
    for c in s2_copies:
        c.start()

    dcol = jnp.transpose(jnp.broadcast_to(dl, (128, slots)))
    dcol = jnp.concatenate([dcol] * (TILE // 128), axis=1)

    @pl.loop(0, htiles)
    def _(j):
        cols = pl.ds(pl.multiple_of(j * TILE, TILE), TILE)
        p = pa[:, cols]
        sig = sigmoid(p)
        gp[:, cols] = (dcol * sw[:, cols].astype(F32) * (sig * (1.0 + p * (1.0 - sig)))).astype(BF16)

    blocks = g.shape[0]
    half, part = blocks // 2, blocks // 4
    mine = core * half
    other = half - mine
    prow = part // htiles * RB

    def pair_copy(k):
        return remote(
            g.at[pl.ds(other + k * part, part)], rc.at[pl.ds(k * part, part)],
            pair_sem.at[0, k], pair_sem.at[1, k], {"tm": partner},
        )

    for k in range(4):
        first = (other if k < 2 else mine) + (k % 2) * part
        r0 = pl.multiple_of(first // htiles * RB, 128)
        for m in range(prow // TILE):
            ltb[...] = jnp.transpose(rr[:, pl.ds(r0 + m * TILE, TILE)])

            @pl.loop(0, htiles)
            def _(j):
                cols = pl.ds(pl.multiple_of(j * TILE, TILE), TILE)
                out = dot(ltb[...], gp[:, cols]).astype(BF16)
                for i in range(TILE // RB):
                    g[first + (m * (TILE // RB) + i) * htiles + j] = out[i * RB : (i + 1) * RB]

        if k < 2:
            pair_copy(k).start()

    def add(dst, dst0, a, a0, b, b0, count):
        step = min(count, 8)

        @pl.loop(0, count // step)
        def _(i):
            o = i * step
            dst[pl.ds(dst0 + o, step)] = (
                a[pl.ds(a0 + o, step)].astype(F32) + b[pl.ds(b0 + o, step)].astype(F32)
            ).astype(BF16)

    def rs(axis, me, n, base, share, right, left, sid, final):
        def dev(p):
            return {"tm": 2 * p + core} if axis == "x" else {"user": p}

        up, down = (me + 1) % n, (me + n - 1) % n

        def to_right(d):
            return remote(
                g.at[pl.ds(base + (me + d) * share, share)], right.at[pl.ds((d - 1) * share, share)],
                rs_sem.at[sid, 0, d], rs_sem.at[sid, 1, d - 1], dev(up),
            )

        def to_left(d):
            return remote(
                g.at[pl.ds(base + (me - d) * share, share)], left.at[pl.ds((d - 1) * share, share)],
                rs_sem.at[sid, 2, d], rs_sem.at[sid, 3, d - 1], dev(down),
            )

        def got(buf, d, lane_id):
            slot = buf.at[pl.ds(d * share, share)]
            remote(slot, slot, rs_sem.at[sid, lane_id - 1, d], rs_sem.at[sid, lane_id, d], dev(up)).wait_recv()

        for d in range(n - 1, 0, -1):
            @pl.when(me + d < n)
            def _():
                if d < n - 1:
                    @pl.when(me > 0)
                    def _():
                        got(right, d, 1)
                        s = base + (me + d) * share
                        add(g, s, g, s, right, d * share, share)
                to_right(d).start()

            @pl.when(me - d >= 0)
            def _():
                if d < n - 1:
                    @pl.when(me < n - 1)
                    def _():
                        got(left, d, 3)
                        s = base + (me - d) * share
                        add(g, s, g, s, left, d * share, share)
                to_left(d).start()
            yield
        own = base + me * share

        @pl.when(me > 0)
        def _():
            got(right, 0, 1)
            add(g, own, g, own, right, 0, share)

        @pl.when(me < n - 1)
        def _():
            got(left, 0, 3)
            add(g, own, g, own, left, 0, share)

        if final:
            res[pl.ds(own, share)] = g[pl.ds(own, share)]
        for d in range(n - 1, 0, -1):
            @pl.when(me + d < n)
            def _():
                to_right(d).wait_send()

            @pl.when(me - d >= 0)
            def _():
                to_left(d).wait_send()
        yield

    def ag(axis, me, n, base, share, sid):
        def dev(p):
            return {"tm": 2 * p + core} if axis == "x" else {"user": p}

        up, down = (me + 1) % n, (me + n - 1) % n

        def move(d, way):
            spot = res.at[pl.ds(base + (me - way * d) * share, share)]
            k = 0 if way > 0 else 2
            return remote(
                spot, spot, ag_sem.at[sid, k, d], ag_sem.at[sid, k + 1, d + 1], dev(up if way > 0 else down)
            )

        def got(d, way):
            spot = res.at[pl.ds(base + (me - way * d) * share, share)]
            k = 0 if way > 0 else 2
            remote(spot, spot, ag_sem.at[sid, k, d], ag_sem.at[sid, k + 1, d], dev(up)).wait_recv()

        for d in range(n):
            @pl.when(me - d >= 0)
            def _():
                if d:
                    got(d, 1)

                if d < n - 1:
                    @pl.when(me < n - 1)
                    def _():
                        move(d, 1).start()

            @pl.when(me + d < n)
            def _():
                if d:
                    got(d, -1)

                if d < n - 1:
                    @pl.when(me > 0)
                    def _():
                        move(d, -1).start()
            yield
        for d in range(n - 1):
            @pl.when((me - d >= 0) & (me < n - 1))
            def _():
                move(d, 1).wait_send()

            @pl.when((me + d < n) & (me > 0))
            def _():
                move(d, -1).wait_send()

    def finish(base, k):
        spot = res.at[pl.ds(base, part)]
        return remote(spot, spot, pair_sem.at[0, 2 + k], pair_sem.at[1, 2 + k], {"tm": partner})

    def stream_a():
        pair_copy(0).wait_recv()
        add(g, mine, g, mine, rc, 0, part)
        sx = part // nx
        sz = sx // nu
        xbase = mine + xi * sx
        yield from rs("x", xi, nx, mine, sx, ax_r, ax_l, 0, False)
        yield from rs("z", us, nu, xbase, sz, az_r, az_l, 1, True)
        yield from ag("z", us, nu, xbase, sz, 0)
        yield from ag("x", xi, nx, mine, sx, 1)
        finish(mine, 0).start()

    def stream_b():
        pair_copy(1).wait_recv()
        base = mine + part
        add(g, base, g, base, rc, part, part)
        sz = part // nu
        sx = sz // nx
        zbase = base + us * sz
        yield from rs("z", us, nu, base, sz, bz_r, bz_l, 2, False)
        yield from rs("x", xi, nx, zbase, sx, bx_r, bx_l, 3, True)
        yield from ag("x", xi, nx, zbase, sx, 2)
        yield from ag("z", us, nu, base, sz, 3)
        finish(base, 1).start()

    def stream_c():
        yield
        for c in s2_copies:
            c.wait_recv()
        total = s2[...]
        for d in range(nt - 1):
            total = total + s2t[d]
        for c in s2_copies:
            c.wait_send()
        s2[...] = total
        more = [
            remote(s2, s2u.at[d - 1], s2_sem.at[2, d - 1], s2_sem.at[3, d - 1], {"user": (us + d) % nu})
            for d in range(1, nu)
        ]
        for c in more:
            c.start()
        for _ in range(3):
            yield
        for c in more:
            c.wait_recv()
        for d in range(nu - 1):
            total = total + s2u[d]
        g2_o[...] = total
        for c in more:
            c.wait_send()

    run_all([stream_a(), stream_b(), stream_c()])
    for k in range(2):
        spot = res.at[pl.ds(other + k * part, part)]
        remote(spot, spot, pair_sem.at[0, 2 + k], pair_sem.at[1, 2 + k], {"tm": partner}).wait_recv()
        finish(mine + k * part, k).wait_send()
        pair_copy(k).wait_send()

    @pl.when(tm < nt - 1)
    def _():
        rim_copy.wait_send()
        for j in range(tiles):
            st_copy(j).wait_send()


def widen(blocks_ref, out_ref):
    htiles = out_ref.shape[1] // TILE
    for b in range(blocks_ref.shape[0]):
        r, c = b // htiles * RB, b % htiles * TILE
        out_ref[r : r + RB, c : c + TILE] = blocks_ref[b].astype(F32)


def body(nt, nu, history, z_weight, xbc_weight, dt_weight, dt_bias, a_log, conv_weight, conv_bias,
         d_skip, norm_gain, out_weight, label_pos, label_count, label_value, item_feat,
         first_weight, second_weight):
    rows, width = history.shape[1:]
    inner, xbc = z_weight.shape[1], xbc_weight.shape[1]
    state = (xbc - inner) // 2
    heads = a_log.shape[0]
    slots = item_feat.shape[1]
    fan, hid = first_weight.shape
    tiles = inner // TILE
    blocks = fan * hid // (RB * TILE)
    part = blocks // 4
    nx = nt // 2
    most = max(nt, nu)

    def vm(shape, dtype=BF16):
        return pltpu.VMEM(shape, dtype)

    slab = (part, RB, TILE)
    scratch = [
        vm((rows, width)), vm((width, inner)), vm((width, xbc)), vm((inner, width)),
        vm((slots, fan)), vm((fan, hid)), vm((16, width)), vm((rows + 8, xbc), F32),
        vm((rows, xbc)), vm((rows, inner)), vm((rows, inner), F32), vm((rows, inner), F32),
        vm((rows, inner), F32), vm((rows, inner)), vm((tiles, state, TILE), F32),
        vm((tiles, state, TILE)), vm((tiles, state, TILE)), vm((rows, inner)),
        vm((slots, hid), F32), vm((slots, hid)), vm((slots, hid)), vm((TILE, slots)),
        vm((blocks, RB, TILE)), vm((blocks // 2, RB, TILE)),
        vm(slab), vm(slab), vm((part // nx, RB, TILE)), vm((part // nx, RB, TILE)),
        vm(slab), vm(slab), vm((part // nu, RB, TILE)), vm((part // nu, RB, TILE)),
        vm((hid // 128, 128), F32), vm((nt - 1, hid // 128, 128), F32), vm((nu - 1, hid // 128, 128), F32),
        pltpu.SemaphoreType.DMA((6,)), pltpu.SemaphoreType.DMA((2,)), pltpu.SemaphoreType.DMA((2, tiles)),
        pltpu.SemaphoreType.DMA((2, 4)), pltpu.SemaphoreType.DMA((4, 4, most)),
        pltpu.SemaphoreType.DMA((4, 4, most + 1)), pltpu.SemaphoreType.DMA((4, most)),
    ]
    hbm, vmem = pl.BlockSpec(memory_space=pl.ANY), pl.BlockSpec(memory_space=pltpu.VMEM)
    enc, logit, grads, second = pl.pallas_call(
        functools.partial(kernel, nt, nu, heads),
        out_shape=(
            jax.ShapeDtypeStruct((rows, width), BF16),
            jax.ShapeDtypeStruct((1, slots), F32),
            jax.ShapeDtypeStruct((blocks, RB, TILE), BF16),
            jax.ShapeDtypeStruct((hid // 128, 128), F32),
        ),
        in_specs=[hbm, hbm, hbm] + [vmem] * 7 + [hbm] + [vmem] * 3 + [hbm, hbm, vmem],
        out_specs=(vmem, vmem, vmem, vmem),
        scratch_shapes=scratch,
        compiler_params=pltpu.CompilerParams(
            collective_id=0, has_side_effects=True, vmem_limit_bytes=56 * 1024 * 1024
        ),
    )(
        history[0], z_weight, xbc_weight, dt_weight, dt_bias[None], a_log[None], conv_weight,
        conv_bias[None], d_skip[None], norm_gain[None], out_weight, label_pos, label_count,
        label_value, item_feat[0], first_weight, second_weight[None],
    )
    steps = 8
    wide = pl.pallas_call(
        widen,
        grid=(steps,),
        out_shape=jax.ShapeDtypeStruct((fan, hid), F32),
        in_specs=[pl.BlockSpec((blocks // steps, RB, TILE), lambda i: (i, 0, 0))],
        out_specs=pl.BlockSpec((fan // steps, hid), lambda i: (i, 0)),
    )(grads)
    return enc[None], logit, wide, second.reshape(hid)


def solution(mesh):
    row = P(("grp", "user"), "tm", None)
    row2 = P(("grp", "user"), "tm")
    in_specs = (row,) + (P(),) * 10 + (row2, row2, row2, row, P(), P())
    out_specs = (row, row2, P("grp", None), P("grp"))
    return jax.shard_map(
        functools.partial(body, mesh.shape["tm"], mesh.shape["user"]),
        mesh=mesh, in_specs=in_specs, out_specs=out_specs, check_vma=False,
    )
```

time: 187 us -> 87.2 us (0.47)
  waiting for transfers between devices: 81.1 us -> 0 us
  Pallas kernels: 0 us -> 79.6 us
  blocking collectives: 21.4 us -> 0 us
  starting transfers between devices: 18.7 us -> 0 us
  matrix products: 17.8 us -> 0 us
  between operations: 15.4 us -> 1.31 us
  local copies, waits for them, and re-layouts: 19.2 us -> 5.93 us
  other arithmetic: 12.8 us -> 0 us
    pallas_call x0 -> x2, Pallas kernels: none -> 79.6 us  [the longest x1 73.5 us: body(): pl.pallas_call(functools.partial(kernel, nt, nu, heads), out_shape=(jax.S...]
    psum x1 -> x0, waiting for transfers between devices: 40.7 us -> none  [body(): lax.psum(share_first.astype(jnp.bfloat16), 'user').astype(jnp.float32)]
    reduce_scatter x1 -> x0, waiting for transfers between devices: 38.9 us -> none  [body(): lax.psum_scatter(grad_one.astype(jnp.bfloat16), 'tm', scatter_dimension=0...]
    ppermute x4 -> x0, starting transfers between devices: 18.6 us -> none  [passed_along(): return lax.ppermute(shard, axis, pairs)]
    dot_general x13 -> x0, matrix products: 17.8 us -> none  [the longest x1 3.01 us: ranker(): jnp.dot(rank_rows.T, grad_pre, preferred_element_type=jnp.float32)]
    psum x1 -> x0, blocking collectives: 10.5 us -> none  [body(): lax.psum(share_second.astype(jnp.bfloat16), 'user').astype(jnp.float32)]
    convert_element_type x8 -> x0, other arithmetic: 7.06 us -> none  [the longest x1 4.07 us: body(): lax.all_gather(summed_first.astype(jnp.bfloat16), 'tm', axis=0, tiled=True)]
    unnamed x1 -> x0, blocking collectives: 5.85 us -> none
  transfers between devices with their start and end apart: 7 -> 0, of which waited for: 4 -> 0; matrix products, arithmetic and copies ran while one was open for 9% -> 0% of each run, Pallas kernels for 0% -> 0%
where the time goes in v1:
time: 87.2 us; the launch traced here: 86.8 us
  Pallas kernels  79.6 us (91%)
  local copies, waits for them, and re-layouts  5.93 us (7%)
  between operations  1.31 us (2%)
    pallas_call x1, Pallas kernels, body(): pl.pallas_call(functools.partial(kernel, nt, nu, heads), out_shape=(jax.S...  73.5 us
    pallas_call x1, Pallas kernels, body(): pl.pallas_call(widen, grid=(steps,), out_shape=jax.ShapeDtypeStruct((fan,...  6.01 us
    unnamed x10, local copies, waits for them, and re-layouts  3.36 us

profile of v1, /device:TPU:0, one launch (start us, length us, event | category | flops | bytes accessed | tf_op | source)
XLA Modules:
  0.0 86.8 jit_solution(18104020599771880903)
XLA Ops:
  1.3 1.3 %broadcast_in_dim.26.sw = bf16[1,1024]{1,0:T(2,128)(2,1)} reshape(bf16[1024]{0:T(1024)(128)(2,1)} %param.33) | data formatting | bytes 4096 | tf_op jit(solution)/shard_map/broadcast_in_dim | solution.py:534
  2.6 1.3 %broadcast_in_dim.23.cb = f32[1,1280]{1,0:T(1,128)} reshape(f32[1280]{0:T(1024)} %param.24) | data formatting | bytes 10240 | tf_op jit(solution)/shard_map/broadcast_in_dim | solution.py:533
  3.8 1.5 %copy.21.dtw = bf16[512,16]{1,0:T(8,128)(2,1)} copy(bf16[512,16]{0,1:T(8,128)(2,1)} %param.20) | data formatting | bytes 32768 | tf_op args[3]
  5.3 73.5 %shard_map.192 = (bf16[256,512]{1,0:T(8,128)(2,1)}, f32[1,512]{1,0:T(1,128)}, bf16[256,16,256]{2,1,0:T(8,128)(2,1)}, f32[8,128]{1,0:T(8,128)}) custom-call(bf16[256,512]{1,0:T(8,128)(2,1)} %bitcast.9, bf16[512,1024]{1,0:T(8,128)(2,1)} %zw.1, bf16[512,1280]{1,0:T(8,128)(2,1)} %xw.1, bf16[512,16]{1,0:T(8,128)(2,1)} %copy.21.dtw, f32[1,16]{1,0:T(1,128)} %bitcast.13, ...), custom_call_target="tpu_custom_call" | custom-call | tf_op jit(solution)/shard_map/pallas_call | solution.py:517
  78.9 0.0 copy-start
  78.9 0.0 copy-start.2
  78.9 0.0 copy-start.1
  78.9 6.0 %shard_map.193 = f32[1024,1024]{1,0:T(8,128)} custom-call(bf16[256,16,256]{2,1,0:T(8,128)(2,1)} %get-tuple-element.10.blocks_ref), custom_call_target="tpu_custom_call" | custom-call | tf_op jit(solution)/shard_map/pallas_call | solution.py:537
  84.9 0.0 copy-done
  84.9 0.7 copy.26
  85.6 0.0 copy-done.2
  85.6 0.6 copy.27
  86.2 0.0 copy-done.1
  86.2 0.6 copy.28
Async XLA Ops:
  78.9 6.0 %copy-start = (bf16[256,512]{1,0:T(8,128)(2,1)S(1)}, bf16[256,512]{1,0:T(8,128)(2,1)}, u32[]{:S(2)}) copy-start(bf16[256,512]{1,0:T(8,128)(2,1)} %get-tuple-element.8) | copy-start | bytes 786436
  78.9 6.7 %copy-start.2 = (f32[1,512]{1,0:T(1,128)S(1)}, f32[1,512]{1,0:T(1,128)}, u32[]{:S(2)}) copy-start(f32[1,512]{1,0:T(1,128)} %get-tuple-element.17) | copy-start | bytes 6148
  78.9 7.3 %copy-start.1 = (f32[8,128]{1,0:T(8,128)S(1)}, f32[8,128]{1,0:T(8,128)}, u32[]{:S(2)}) copy-start(f32[8,128]{1,0:T(8,128)} %get-tuple-element.11) | copy-start | bytes 12292

commit v2 on v1

--- a/solution.py
+++ b/solution.py
@@ -22,14 +22,9 @@
     return jax.nn.sigmoid(v)
 
 
-def run_all(streams):
-    live = list(streams)
-    while live:
-        for s in list(live):
-            try:
-                next(s)
-            except StopIteration:
-                live.remove(s)
+def advance(stream, steps):
+    for _ in range(steps):
+        next(stream, None)
 
 
 def kernel(
@@ -87,9 +82,9 @@
         rim[...] = jnp.zeros_like(rim)
         st_in[...] = jnp.zeros_like(st_in)
 
-    v = dot(hv[...], dtw[...]) + dtb[...]
+    v = dot(hv[...], dtw[...], ((1,), (1,))) + dtb[...].reshape(1, head_count)
     dt = jnp.maximum(v, 0.0) + jnp.log1p(jnp.exp(-jnp.abs(v)))
-    log_decay = -jnp.exp(alog[...]) * dt
+    log_decay = -jnp.exp(alog[...].reshape(1, head_count)) * dt
     ri = lax.broadcasted_iota(jnp.int32, (rows, rows), 0)
     ci = lax.broadcasted_iota(jnp.int32, (rows, rows), 1)
     tri = jnp.where(ci <= ri, 1.0, 0.0).astype(F32)
@@ -103,7 +98,7 @@
     last = cum[rows - 1 : rows, :]
     ea[...] = dot(jnp.exp(cum), spread, precision=HIGH)
     eb[...] = dot(jnp.exp(last - cum) * dt, spread, precision=HIGH)
-    skip = dot(jnp.broadcast_to(dsk[...], (8, head_count)), spread, precision=HIGH)[0:1]
+    skip = dot(jnp.broadcast_to(dsk[...].reshape(1, head_count), (8, head_count)), spread, precision=HIGH)[0:1]
 
     loads[1].wait()
 
@@ -122,7 +117,7 @@
         edge = dot(rim[...], xv[:, cols]).astype(BF16).astype(F32)
         rawf[pl.ds(0, 8), cols] = edge[8:16]
         taps = cw.shape[0]
-        acc = jnp.broadcast_to(cb[:, cols], (rows, TILE))
+        acc = jnp.broadcast_to(cb[cols].reshape(1, TILE), (rows, TILE))
         for k in range(taps):
             acc = acc + cw[pl.ds(k, 1), cols] * rawf[pl.ds(8 - (taps - 1) + k, rows), cols]
         xb[:, cols] = (acc * sigmoid(acc)).astype(BF16)
@@ -201,7 +196,7 @@
     scale = lax.rsqrt(square / inner + 1e-05)
     for j in range(tiles):
         cols = slice(j * TILE, (j + 1) * TILE)
-        nb[:, cols] = (y[:, cols] * scale * ng[:, cols]).astype(BF16)
+        nb[:, cols] = (y[:, cols] * scale * ng[cols].reshape(1, TILE)).astype(BF16)
     loads[5].wait()
 
     @pl.loop(0, width // TILE)
@@ -221,7 +216,7 @@
         pa[:, cols] = p
         hb[:, cols] = (p * sigmoid(p)).astype(BF16)
 
-    logit = dot(jnp.broadcast_to(sw[...], (16, hid)), hb[...], ((1,), (1,)))[0:1]
+    logit = dot(jnp.broadcast_to(sw[...].astype(F32).reshape(1, hid), (16, hid)).astype(BF16), hb[...], ((1,), (1,)))[0:1]
     live = (lax.broadcasted_iota(jnp.int32, (1, slots), 1) < cnt[...]).astype(F32)
     logit_o[...] = live * logit
     dl = live * (sigmoid(logit) - lab[...].astype(F32))
@@ -248,7 +243,7 @@
         cols = pl.ds(pl.multiple_of(j * TILE, TILE), TILE)
         p = pa[:, cols]
         sig = sigmoid(p)
-        gp[:, cols] = (dcol * sw[:, cols].astype(F32) * (sig * (1.0 + p * (1.0 - sig)))).astype(BF16)
+        gp[:, cols] = (dcol * sw[cols].astype(F32).reshape(1, TILE) * (sig * (1.0 + p * (1.0 - sig)))).astype(BF16)
 
     blocks = g.shape[0]
     half, part = blocks // 2, blocks // 4
@@ -287,6 +282,8 @@
             dst[pl.ds(dst0 + o, step)] = (
                 a[pl.ds(a0 + o, step)].astype(F32) + b[pl.ds(b0 + o, step)].astype(F32)
             ).astype(BF16)
+
+    later = []
 
     def rs(axis, me, n, base, share, right, left, sid, final):
         def dev(p):
@@ -345,14 +342,18 @@
 
         if final:
             res[pl.ds(own, share)] = g[pl.ds(own, share)]
-        for d in range(n - 1, 0, -1):
-            @pl.when(me + d < n)
-            def _():
-                to_right(d).wait_send()
-
-            @pl.when(me - d >= 0)
-            def _():
-                to_left(d).wait_send()
+
+        def drain():
+            for d in range(n - 1, 0, -1):
+                @pl.when(me + d < n)
+                def _():
+                    to_right(d).wait_send()
+
+                @pl.when(me - d >= 0)
+                def _():
+                    to_left(d).wait_send()
+
+        later.append(drain)
         yield
 
     def ag(axis, me, n, base, share, sid):
@@ -394,14 +395,18 @@
                     def _():
                         move(d, -1).start()
             yield
-        for d in range(n - 1):
-            @pl.when((me - d >= 0) & (me < n - 1))
-            def _():
-                move(d, 1).wait_send()
-
-            @pl.when((me + d < n) & (me > 0))
-            def _():
-                move(d, -1).wait_send()
+
+        def drain():
+            for d in range(n - 1):
+                @pl.when((me - d >= 0) & (me < n - 1))
+                def _():
+                    move(d, 1).wait_send()
+
+                @pl.when((me + d < n) & (me > 0))
+                def _():
+                    move(d, -1).wait_send()
+
+        later.append(drain)
 
     def finish(base, k):
         spot = res.at[pl.ds(base, part)]
@@ -433,7 +438,6 @@
         finish(base, 1).start()
 
     def stream_c():
-        yield
         for c in s2_copies:
             c.wait_recv()
         total = s2[...]
@@ -448,8 +452,7 @@
         ]
         for c in more:
             c.start()
-        for _ in range(3):
-            yield
+        yield
         for c in more:
             c.wait_recv()
         for d in range(nu - 1):
@@ -458,7 +461,23 @@
         for c in more:
             c.wait_send()
 
-    run_all([stream_a(), stream_b(), stream_c()])
+    sa, sb, sc = stream_a(), stream_b(), stream_c()
+    advance(sa, nx - 1)
+    advance(sb, nu)
+    advance(sa, 1)
+    advance(sb, nx - 1)
+    advance(sa, nu)
+    advance(sc, 1)
+    advance(sb, 2)
+    advance(sa, nu)
+    advance(sb, nx - 1)
+    advance(sa, 1)
+    advance(sb, nu)
+    advance(sa, nx)
+    advance(sb, 1)
+    advance(sc, 1)
+    for drain in later:
+        drain()
     for k in range(2):
         spot = res.at[pl.ds(other + k * part, part)]
         remote(spot, spot, pair_sem.at[0, 2 + k], pair_sem.at[1, 2 + k], {"tm": partner}).wait_recv()
@@ -472,11 +491,31 @@
             st_copy(j).wait_send()
 
 
-def widen(blocks_ref, out_ref):
-    htiles = out_ref.shape[1] // TILE
-    for b in range(blocks_ref.shape[0]):
-        r, c = b // htiles * RB, b % htiles * TILE
-        out_ref[r : r + RB, c : c + TILE] = blocks_ref[b].astype(F32)
+def widen(chunks, enc, logit, second, grads, enc_o, logit_o, second_o, wide_o, held, wide, in_sem, out_sem):
+    blocks, rows = grads.shape[0] // chunks, wide_o.shape[0] // chunks
+    htiles = wide_o.shape[1] // TILE
+    small = [
+        pltpu.make_async_copy(a, b, out_sem.at[chunks + i])
+        for i, (a, b) in enumerate(((enc, enc_o), (logit, logit_o), (second, second_o)))
+    ]
+    ins = [
+        pltpu.make_async_copy(grads.at[pl.ds(k * blocks, blocks)], held.at[k], in_sem.at[k])
+        for k in range(chunks)
+    ]
+    outs = [
+        pltpu.make_async_copy(wide.at[k], wide_o.at[pl.ds(k * rows, rows)], out_sem.at[k])
+        for k in range(chunks)
+    ]
+    for c in ins + small:
+        c.start()
+    for k in range(chunks):
+        ins[k].wait()
+        for b in range(blocks):
+            r, c = b // htiles * RB, b % htiles * TILE
+            wide[k, r : r + RB, c : c + TILE] = held[k, b].astype(F32)
+        outs[k].start()
+    for c in outs + small:
+        c.wait()
 
 
 def body(nt, nu, history, z_weight, xbc_weight, dt_weight, dt_bias, a_log, conv_weight, conv_bias,
@@ -529,18 +568,27 @@
             collective_id=0, has_side_effects=True, vmem_limit_bytes=56 * 1024 * 1024
         ),
     )(
-        history[0], z_weight, xbc_weight, dt_weight, dt_bias[None], a_log[None], conv_weight,
-        conv_bias[None], d_skip[None], norm_gain[None], out_weight, label_pos, label_count,
-        label_value, item_feat[0], first_weight, second_weight[None],
+        history[0], z_weight, xbc_weight, dt_weight.T, dt_bias, a_log, conv_weight,
+        conv_bias, d_skip, norm_gain, out_weight, label_pos, label_count,
+        label_value, item_feat[0], first_weight, second_weight,
     )
-    steps = 8
-    wide = pl.pallas_call(
-        widen,
-        grid=(steps,),
-        out_shape=jax.ShapeDtypeStruct((fan, hid), F32),
-        in_specs=[pl.BlockSpec((blocks // steps, RB, TILE), lambda i: (i, 0, 0))],
-        out_specs=pl.BlockSpec((fan // steps, hid), lambda i: (i, 0)),
-    )(grads)
+    chunks = 8
+    enc, logit, second, wide = pl.pallas_call(
+        functools.partial(widen, chunks),
+        out_shape=(
+            jax.ShapeDtypeStruct((rows, width), BF16),
+            jax.ShapeDtypeStruct((1, slots), F32),
+            jax.ShapeDtypeStruct((hid // 128, 128), F32),
+            jax.ShapeDtypeStruct((fan, hid), F32),
+        ),
+        in_specs=[hbm] * 4,
+        out_specs=(hbm,) * 4,
+        scratch_shapes=[
+            vm((chunks, blocks // chunks, RB, TILE)), vm((chunks, fan // chunks, hid), F32),
+            pltpu.SemaphoreType.DMA((chunks,)), pltpu.SemaphoreType.DMA((chunks + 3,)),
+        ],
+        compiler_params=pltpu.CompilerParams(vmem_limit_bytes=56 * 1024 * 1024),
+    )(enc, logit, second, grads)
     return enc[None], logit, wide, second.reshape(hid)
 
 

time: 87.2 us -> 89.7 us (1.029); the launches traced: 86.8 us -> 88.2 us
  Pallas kernels: 79.6 us -> 86.9 us
  local copies, waits for them, and re-layouts: 5.93 us -> 0 us
    pallas_call x1, Pallas kernels: 73.5 us -> 77.5 us  [body(): pl.pallas_call(functools.partial(kernel, nt, nu, heads), out_shape=(jax.S...]
    pallas_call x1, Pallas kernels: 6.01 us -> 9.41 us  [body(): pl.pallas_call(functools.partial(widen, chunks), out_shape=(jax.ShapeDtyp...]
    unnamed x10 -> x0, local copies, waits for them, and re-layouts: 3.36 us -> none
    broadcast_in_dim x2 -> x0, local copies, waits for them, and re-layouts: 2.57 us -> none  [the longest x1 1.29 us: body(): conv_bias[None]]
where the time goes in v2:
time: 89.7 us; the launch traced here: 88.2 us
  Pallas kernels  86.9 us (97%)
  between operations  1.29 us (1%)
    pallas_call x1, Pallas kernels, body(): pl.pallas_call(functools.partial(kernel, nt, nu, heads), out_shape=(jax.S...  77.5 us
    pallas_call x1, Pallas kernels, body(): pl.pallas_call(functools.partial(widen, chunks), out_shape=(jax.ShapeDtyp...  9.41 us

profile of v2, /device:TPU:0, one launch (start us, length us, event | category | flops | bytes accessed | tf_op | source)
XLA Modules:
  0.0 88.2 jit_solution(1358388696845805652)
XLA Ops:
  1.3 77.5 %shard_map.192 = (bf16[256,512]{1,0:T(8,128)(2,1)}, f32[1,512]{1,0:T(1,128)}, bf16[256,16,256]{2,1,0:T(8,128)(2,1)}, f32[8,128]{1,0:T(8,128)}) custom-call(bf16[256,512]{1,0:T(8,128)(2,1)} %bitcast.6, bf16[512,1024]{1,0:T(8,128)(2,1)} %zw.1, bf16[512,1280]{1,0:T(8,128)(2,1)} %xw.1, bf16[16,512]{1,0:T(8,128)(2,1)} %bitcast.7, f32[16]{0:T(128)} %dtb.1, ...), custom_call_target="tpu_custom_call" | custom-call | tf_op jit(solution)/shard_map/pallas_call | solution.py:556
  78.8 9.4 %shard_map.193 = (bf16[256,512]{1,0:T(8,128)(2,1)}, f32[1,512]{1,0:T(1,128)}, f32[8,128]{1,0:T(8,128)}, f32[1024,1024]{1,0:T(8,128)}) custom-call(bf16[256,512]{1,0:T(8,128)(2,1)} %get-tuple-element.12.enc, f32[1,512]{1,0:T(1,128)} %get-tuple-element.13.logit, f32[8,128]{1,0:T(8,128)} %get-tuple-element.14.second, bf16[256,16,256]{2,1,0:T(8,128)(2,1)} %get-tuple-element.15.grads), custom_call_target="tpu_custom_call" | custom-call | tf_op jit(solution)/shard_map/pallas_call | solution.py:576
